TPU v7x, 256 devices: a whole 4x4x8 slice. The times are simulated.
256 devices in a mesh: fsdp: 16 (over z_hi, x, core), expert: 16 (over z_lo, y).
Axes of the slice: x: 4, y: 4, z: 8 (z_hi: 2, z_lo: 4; z = z_hi * 4 + z_lo), core: 2. Of those that a mesh axis runs over, the one named last changes fastest.
Arguments:
- out_grad: bfloat16 [32768, 4096], P(('fsdp', 'expert')), may hold values from -1.5 to 1.5
- router_probs: bfloat16 [32768, 8], P(('fsdp', 'expert')), may hold values from 0.049804688 to 0.59765625
- expert_ids: int32 [32768, 8], P(('fsdp', 'expert')), may hold values from 0 to 127, as said below
- saved_hidden: bfloat16 [16, 16, 256, 2048], P('fsdp', 'expert'), may hold values from -6 to 6
- w_down: bfloat16 [16, 4096, 1024], P('expert', 'fsdp'), may hold values from -0.1875 to 0.1875
Outputs:
- dprobs: float32 [32768, 8], P(('fsdp', 'expert'))
- grad_pre: bfloat16 [16, 16, 256, 2048], P('fsdp', 'expert')
- grad_down: float32 [16, 4096, 1024], P('expert', 'fsdp')
Inputs may be any that keep to these rules, and one draw needn't show every extreme that they name: `expert_ids`: each row names 8 different experts. In every aligned block of 128 rows (the tokens of one device) some expert below 16 is named by 16 rows or more.
All inputs are finite; a program needn't handle non-finite values.
Results may differ from a plain program's by a relative error of at most 0.01.
Values may be sent and summed in bfloat16 or wider, within the bound.
A program may use at most 128 MiB of HBM per device.

v0:
```python
import jax
import jax.numpy as jnp
from jax import lax
from jax.sharding import PartitionSpec as P

CAP = 16


def route_block(block_ids, experts, capacity):
    flat_ids = block_ids.reshape(-1)
    onehot = (flat_ids[:, None] == jnp.arange(experts, dtype=jnp.int32)[None, :]).astype(jnp.int32)
    before = jnp.sum((jnp.cumsum(onehot, axis=0) - onehot) * onehot, axis=1)
    is_kept = (flat_ids < experts) & (before < capacity)
    slot_of = jnp.where(is_kept, flat_ids * capacity + before, experts * capacity)
    source = jnp.arange(flat_ids.shape[0], dtype=jnp.int32)
    row_of = jnp.zeros((experts * capacity,), jnp.int32).at[slot_of].set(source, mode="drop")
    filled = (
        jnp.zeros((experts * capacity,), jnp.int32)
        .at[slot_of]
        .set(jnp.ones_like(source), mode="drop")
    )
    return (slot_of, row_of, filled)


def make_row_fold(routed, segment):
    return jnp.dot(routed, segment, preferred_element_type=jnp.float32)


def per_device(out_grad, router_probs, expert_ids, saved_hidden, w_down):
    experts = lax.axis_size("expert")
    width = out_grad.shape[1]
    hidden_width = w_down.shape[2]
    picks = expert_ids.shape[1]
    slot_of, row_of, filled = route_block(expert_ids, experts, CAP)
    live = filled.astype(jnp.bfloat16)
    send_rows = (out_grad[row_of // picks] * live[:, None]).reshape(experts, CAP, width)
    send_probs = (router_probs.reshape(-1)[row_of] * live).reshape(experts, CAP)
    routed, weight = (
        lax.all_to_all(send_rows, "expert", split_axis=0, concat_axis=0, tiled=True),
        lax.all_to_all(send_probs, "expert", split_axis=0, concat_axis=0, tiled=True),
    )
    routed = routed.reshape(-1, width)
    weight = weight.reshape(-1)
    hidden = saved_hidden[0, 0]
    gate_pre = hidden[:, :hidden_width].astype(jnp.float32)
    up_pre = hidden[:, hidden_width:].astype(jnp.float32)
    sigma = jax.nn.sigmoid(gate_pre)
    activation = (gate_pre * sigma * up_pre).astype(jnp.bfloat16)
    probs_col = weight.astype(jnp.float32)[:, None]
    scaled = (probs_col * routed.astype(jnp.float32)).astype(jnp.bfloat16)
    local_rows = w_down[0]
    back_grad = make_row_fold(routed, lax.all_gather(local_rows, "fsdp", axis=0, tiled=True))
    grad_down = lax.psum_scatter(
        lax.dot_general(
            scaled, activation, (((0,), (0,)), ((), ())), preferred_element_type=jnp.float32
        ),
        "fsdp",
        scatter_dimension=0,
        tiled=True,
    )
    slot_grad = jnp.sum(activation.astype(jnp.float32) * back_grad, axis=1)
    grad_hidden = probs_col * back_grad
    grad_gate = grad_hidden * up_pre * sigma * (1.0 + gate_pre * (1.0 - sigma))
    grad_up = grad_hidden * gate_pre * sigma
    grad_pre = jnp.concatenate([grad_gate, grad_up], axis=1).astype(jnp.bfloat16)
    returned = lax.all_to_all(
        slot_grad.reshape(experts, CAP), "expert", split_axis=0, concat_axis=0, tiled=True
    ).reshape(-1)
    safe = jnp.minimum(slot_of, experts * CAP - 1)
    dprobs = jnp.where(slot_of < experts * CAP, returned[safe], jnp.zeros((), jnp.float32)).reshape(
        expert_ids.shape
    )
    return (dprobs, grad_pre[None, None], grad_down[None])


def solution(mesh):
    placed = (
        P(("fsdp", "expert"), None),
        P(("fsdp", "expert"), None),
        P(("fsdp", "expert"), None),
        P("fsdp", "expert", None, None),
        P("expert", "fsdp", None),
    )
    return jax.shard_map(
        per_device,
        mesh=mesh,
        in_specs=placed,
        out_specs=(
            P(("fsdp", "expert"), None),
            P("fsdp", "expert", None, None),
            P("expert", "fsdp", None),
        ),
        check_vma=False,
    )
```

profile of v0, /device:TPU:1, one launch (start us, length us, event | category | flops | bytes accessed | tf_op | source)
XLA Modules:
  0.0 377.2 jit_solution(12557077250267261202)
XLA Ops:
  7.2 0.7 all-gather.3.cloned.1.call-update
  7.9 0.8 copy.18
  8.9 0.8 copy.24
  9.9 4.5 %reduce-window.6 = s32[16,8,128]{2,1,0:T(8,128)S(1)} reduce-window(s32[16,8,128]{2,1,0:T(8,128)S(1)} %fusion.19, s32[]{:T(128)} %constant.13.clone.1), window={size=1x1x128 pad=0_0x0_0x127_0}, to_apply=%region_0.0 | reduce-window | flops 2080768 | bytes 131076 | tf_op jit(solution)/shard_map/reduce-window
  15.1 4.3 %scatter_custom_fusion.1 = s32[256]{0:T(256)S(1)} fusion(s32[1024]{0:T(1024)S(1)} %bitcast.46, s32[1024]{0:T(1024)S(1)} %broadcast.134, s32[]{:T(128)} %constant.13.clone.1), kind=kCustom, calls=%fused_computation.56 | custom fusion | bytes 1028 | tf_op jit(solution)/shard_map/scatter | solution.py:20
  19.4 4.3 %scatter_custom_fusion = s32[256]{0:T(256)S(1)} fusion(s32[1024]{0:T(1024)S(1)} %bitcast.47, s32[1024]{0:T(1024)S(1)} %iota.11, s32[]{:T(128)} %constant.13.clone.1), kind=kCustom, calls=%fused_computation.58 | custom fusion | bytes 1028 | tf_op jit(solution)/shard_map/scatter | solution.py:16
  23.7 1.9 gather_fusion.2
  25.7 0.7 all_to_all.20
  26.4 9.2 %all-to-all-start.2 = ((bf16[16,1,16]{2,1,0:T(2,128)(2,1)}), bf16[16,1,16]{2,1,0:T(2,128)(2,1)S(1)}, u32[]{:S(2)}, u32[]{:S(2)}) async-start(bf16[16,1,16]{2,1,0:T(2,128)(2,1)} %all_to_all.20), calls=%async_computation.2 | async-start | bytes 16384 | tf_op jit(solution)/shard_map/all_to_all | solution.py:40
  35.6 1.9 gather_fusion
  37.5 1.6 broadcast_multiply_fusion
  39.1 3.5 all-to-all-done.2
  42.6 3.7 all-to-all-start
  46.5 86.1 %all-to-all-done = bf16[16,16,4096]{2,1,0:T(8,128)(2,1)S(1)} async-done(((bf16[16,16,4096]{2,1,0:T(8,128)(2,1)}), bf16[16,16,4096]{2,1,0:T(8,128)(2,1)S(1)}, u32[]{:S(2)}, u32[]{:S(2)}) %all-to-all-start) | async-done | bytes 2097184 | tf_op jit(solution)/shard_map/all_to_all | solution.py:39
  132.6 9.8 %fusion.2 = f32[4096,1024]{1,0:T(8,128)} fusion(bf16[256,4096]{1,0:T(8,128)(2,1)S(1)} %bitcast.37, f32[256]{0:T(256)S(1)} %reshape.168, bf16[256,2048]{1,0:T(8,128)(2,1)} %bitcast.40), kind=kOutput, calls=%fused_computation.8 | convolution fusion | flops 2152726528 | bytes 19923968 | tf_op jit(solution)/shard_map/dot_general | solution.py:54
  142.5 7.6 %fusion.15 = (bf16[1,1,256,1024]{3,2,1,0:T(8,128)(2,1)}, bf16[1,1,256,1024]{3,2,1,0:T(8,128)(2,1)}, f32[256]{0:T(256)S(1)}) fusion(f32[256]{0:T(256)S(1)} %reshape.168, bf16[256,2048]{1,0:T(8,128)(2,1)} %bitcast.41, bf16[256,4096]{1,0:T(8,128)(2,1)S(1)} %bitcast.38, bf16[1,4096,1024]{2,1,0:T(8,128)(2,1)} %all-gather.3.cloned.1.call-done), kind=kOutput, calls=%fused_computation.30 | convolution fusion | flops 2153250560 | bytes 12584960 | tf_op jit(solution)/shard_map/dot_general | solution.py:26
  150.1 0.7 all_to_all.16
  150.8 10.7 %all-to-all-start.1 = ((f32[16,1,16]{2,1,0:T(1,128)}), f32[16,1,16]{2,1,0:T(1,128)S(1)}, u32[]{:S(2)}, u32[]{:S(2)}) async-start(f32[16,1,16]{2,1,0:T(1,128)} %all_to_all.16), calls=%async_computation.1 | async-start | bytes 16384 | tf_op jit(solution)/shard_map/all_to_all | solution.py:66
  161.5 2.4 pad_maximum_fusion
  163.9 4.4 %all-to-all-done.1 = f32[16,1,16]{2,1,0:T(1,128)S(1)} async-done(((f32[16,1,16]{2,1,0:T(1,128)}), f32[16,1,16]{2,1,0:T(1,128)S(1)}, u32[]{:S(2)}, u32[]{:S(2)}) %all-to-all-start.1) | async-done | bytes 1056 | tf_op jit(solution)/shard_map/all_to_all | solution.py:66
  168.8 0.7 reduce.7
  169.5 6.8 %gather_fusion.1 = f32[1024]{0:T(1024)S(1)} fusion(f32[256]{0:T(256)S(1)} %reshape.166, s32[1024]{0:T(1024)S(1)} %broadcast_clamp_fusion), kind=kCustom, calls=%fused_computation.1 | custom fusion | bytes 12288 | tf_op jit(solution)/shard_map/gather | solution.py:70
  176.5 0.7 copy.26
  177.2 193.2 %reduce-scatter.2.cloned.1.call-done = f32[256,1024]{1,0:T(8,128)} async-done(((f32[4096,1024]{1,0:T(8,128)}), f32[256,1024]{1,0:T(8,128)}) %reduce-scatter.2.cloned.1.call-update) | async-done | bytes 1048592 | tf_op jit(solution)/shard_map/reduce_scatter | solution.py:53
  (37 shorter events, 2.1 us)
Async XLA Ops:
  7.2 28.5 %copy-start = (bf16[128,4096]{1,0:T(8,128)(2,1)S(1)}, bf16[128,4096]{1,0:T(8,128)(2,1)}, u32[]{:S(2)}) copy-start(bf16[128,4096]{1,0:T(8,128)(2,1)} %param.5) | copy-start | bytes 3145732
  7.2 135.4 %all-gather.3.cloned.1.call-start = ((), (), s32[]{:S(2)}) async-start(), calls=%async_computation.5 | async-start | bytes 8912896 | tf_op jit(solution)/shard_map/all_gather | solution.py:52
  26.4 16.2 %all-to-all-start.2 = ((bf16[16,1,16]{2,1,0:T(2,128)(2,1)}), bf16[16,1,16]{2,1,0:T(2,128)(2,1)S(1)}, u32[]{:S(2)}, u32[]{:S(2)}) async-start(bf16[16,1,16]{2,1,0:T(2,128)(2,1)} %all_to_all.20), calls=%async_computation.2 | async-start | bytes 16384 | tf_op jit(solution)/shard_map/all_to_all | solution.py:40
  42.6 90.0 %all-to-all-start = ((bf16[16,16,4096]{2,1,0:T(8,128)(2,1)}), bf16[16,16,4096]{2,1,0:T(8,128)(2,1)S(1)}, u32[]{:S(2)}, u32[]{:S(2)}) async-start(bf16[16,16,4096]{2,1,0:T(8,128)(2,1)} %broadcast_multiply_fusion), calls=%async_computation | async-start | bytes 4194304 | tf_op jit(solution)/shard_map/all_to_all | solution.py:39
  46.3 324.1 %reduce-scatter.2.cloned.1.call-start = ((), (), s32[]{:S(2)}) async-start(), calls=%async_computation.4 | async-start | bytes 17825792 | tf_op jit(solution)/shard_map/reduce_scatter | solution.py:53
  150.8 17.5 %all-to-all-start.1 = ((f32[16,1,16]{2,1,0:T(1,128)}), f32[16,1,16]{2,1,0:T(1,128)S(1)}, u32[]{:S(2)}, u32[]{:S(2)}) async-start(f32[16,1,16]{2,1,0:T(1,128)} %all_to_all.16), calls=%async_computation.1 | async-start | bytes 16384 | tf_op jit(solution)/shard_map/all_to_all | solution.py:66
Sparse Core Ops, SparseCore 0:
  10.7 131.7 all-gather.2
  147.8 222.5 reduce-scatter.1
where the time goes:
time: 378 us; the launch traced here: 377 us
  waiting for transfers between devices  288 us (76%)
  local copies, waits for them, and re-layouts  24.6 us (7%)
  starting transfers between devices  23.7 us (6%)
  matrix products  17.3 us (5%)
  between operations  14.3 us (4%)
  other arithmetic  9.38 us (2%)
    reduce_scatter x1, waiting for transfers between devices, per_device(): lax.psum_scatter(lax.dot_general(scaled, activation, (((0,), (0,)), ((),...  193 us
    all_to_all x1, waiting for transfers between devices, per_device(): lax.all_to_all(send_rows, 'expert', split_axis=0, concat_axis=0, tiled=True)  86.1 us
    all_to_all x1, starting transfers between devices, per_device(): lax.all_to_all(slot_grad.reshape(experts, CAP), 'expert', split_axis=0, c...  10.7 us
    dot_general x1, matrix products, per_device(): lax.dot_general(scaled, activation, (((0,), (0,)), ((), ())), preferred_e...  9.76 us
    all_to_all x1, starting transfers between devices, per_device(): lax.all_to_all(send_probs, 'expert', split_axis=0, concat_axis=0, tiled=T...  9.19 us
  transfers between devices with their start and end apart: 5, of which 4 were waited for; matrix products, arithmetic and copies ran while one was open for 13% of the time, Pallas kernels for 0%

commit v1 on v0

v1 whole, which is shorter than its diff:
```python
import jax
import jax.numpy as jnp
from jax import lax
from jax.experimental import pallas as pl
from jax.experimental.pallas import tpu as pltpu
from jax.sharding import PartitionSpec as P

F32 = jnp.float32
BF16 = jnp.bfloat16
MESH = pl.DeviceIdType.MESH
CAP = 16
NX = 4
STAGES = ((0, 0, 4), (1, 2, 1), (1, 1, 1), (1, 3, 1), (1, 0, 1))
WSTAGE = len(STAGES)


def kernel(
    ids_ref, probs_ref, og_hbm, hid_hbm, w_hbm,
    dp_out, gp_out, gd_out,
    meta, ogb, gbuf, wsend, wbuf, sendbuf, routed, hidv, act, bvec, wq, sct, pown,
    csend, crecv, zsend, zrecv, bp, bsend, brecv, sgb, ret,
    hid_sem, meta_s, meta_r, og_s, og_r, w_s, w_r, act_s, act_r, a_s, a_r,
    c_s, c_r, z_s, z_r, b_s, b_r, ret_s, ret_r,
):
    ne = 16
    f = lax.axis_index("fsdp")
    e = lax.axis_index("expert")
    zh, x, c = f // 8, (f // 2) % 4, f % 2

    def at_x(d):
        return (zh * 8 + ((x + d) % 4) * 2 + c, e)

    z_peer = ((1 - zh) * 8 + x * 2 + c, e)
    sibling = (zh * 8 + x * 2 + 1 - c, e)

    def remote(src, dst, ss, rs, dev):
        return pltpu.make_async_remote_copy(
            src_ref=src, dst_ref=dst, send_sem=ss, recv_sem=rs, device_id=dev, device_id_type=MESH
        )

    def drain(ref, sem):
        pltpu.make_async_copy(ref, ref, sem).wait()

    own_w = pltpu.make_async_copy(w_hbm, wq.at[:, pl.ds(0, 128), :], w_r.at[0])
    own_hid = pltpu.make_async_copy(hid_hbm, hidv, hid_sem)

    def og_columns(xt, b):
        dz, dc = b % 2, b // 2
        col = ((zh + dz) % 2) * 2048 + xt * 512 + ((c + dc) % 2) * 256
        return og_hbm.at[:, pl.ds(pl.multiple_of(col, 256), 256)]

    for b in range(4):
        pltpu.make_async_copy(og_columns(x, b), ogb.at[0, b], og_r.at[0]).start()
    own_hid.start()
    own_w.start()
    meta[0, 0:8, :] = ids_ref[...].astype(F32)
    meta[0, 8:16, :] = probs_ref[...].astype(F32)

    barrier = pltpu.get_barrier_semaphore()
    for d in (1, 2, 3):
        pl.semaphore_signal(barrier, inc=1, device_id=at_x(d), device_id_type=MESH)
    pl.semaphore_signal(barrier, inc=1, device_id=z_peer, device_id_type=MESH)
    pl.semaphore_signal(barrier, inc=1, device_id=sibling, device_id_type=MESH)

    def greet(k, carry):
        pl.semaphore_signal(barrier, inc=1, device_id=(f, (e + k) % ne), device_id_type=MESH)
        return carry

    lax.fori_loop(1, ne, greet, 0)
    pl.semaphore_wait(barrier, 5 + ne - 1)

    for d in (2, 1, 3):
        remote(meta.at[0], meta.at[4 - d], meta_s.at[d], meta_r.at[4 - d], at_x(d)).start()
    for d in (2, 1, 3):
        for b in range(4):
            remote(
                og_columns((x + d) % 4, b), ogb.at[4 - d, b], og_s.at[d], og_r.at[4 - d], at_x(d)
            ).start()
    remote(w_hbm, wq.at[:, pl.ds(128, 128), :], w_s.at[0], w_r.at[1], z_peer).start()
    remote(w_hbm, wq.at[:, pl.ds(256, 128), :], w_s.at[1], w_r.at[2], sibling).start()

    tri_r = lax.broadcasted_iota(jnp.int32, (128, 128), 0)
    tri_c = lax.broadcasted_iota(jnp.int32, (128, 128), 1)
    upper = jnp.where(tri_r < tri_c, 1.0, 0.0).astype(BF16)
    e_iota = lax.broadcasted_iota(jnp.int32, (ne, 128), 0).astype(F32)
    r_iota = lax.broadcasted_iota(jnp.int32, (ne, CAP, 128), 1).astype(F32)
    lane = lax.broadcasted_iota(jnp.int32, (ne * CAP, 128), 1)
    wacc = jnp.zeros((ne * CAP, 128), F32)
    for d in (0, 1, 3, 2):
        if d:
            drain(meta.at[d], meta_r.at[d])
        ids8 = meta[d, 0:8, :]
        pr8 = meta[d, 8:16, :]
        named = jnp.zeros((ne, 128), F32)
        prob = jnp.zeros((ne, 128), F32)
        for k in range(8):
            hit = ids8[k : k + 1, :] == e_iota
            named = named + jnp.where(hit, 1.0, 0.0)
            prob = prob + jnp.where(hit, pr8[k : k + 1, :], 0.0)
        rank = jnp.dot(named.astype(BF16), upper, preferred_element_type=F32)
        rank = jnp.where(named > 0.0, rank, -1.0)
        pick = jnp.where(rank[:, None, :] == r_iota, 1.0, 0.0)
        wcol = jnp.sum((pick * prob[:, None, :]).reshape(ne * CAP, 128), axis=1, keepdims=True)
        wacc = jnp.where(lane == d, wcol, wacc)
        gbuf[d] = pick.reshape(ne * CAP, 128).astype(BF16)
    wsend[...] = wacc.astype(BF16)

    for d in (0, 1, 3, 2):
        drain(ogb.at[d], og_r.at[d])
        g = gbuf[d]
        for b in range(4):
            rows = jnp.dot(g, ogb[d, b], preferred_element_type=F32).astype(BF16)
            sendbuf[0, d, :, b * 128 : b * 128 + 128] = rows[:, :128]
            sendbuf[1, d, :, b * 128 : b * 128 + 128] = rows[:, 128:]

    def my_rows(ref, h, d0, dn, who):
        return ref.at[h, pl.ds(d0, dn), pl.ds(pl.multiple_of(who * CAP, CAP), CAP), :]

    def wrows(ref, who):
        return ref.at[pl.ds(pl.multiple_of(who * CAP, CAP), CAP), :]

    def exchange(first, count):
        for i in range(first, first + count):
            h, d0, dn = STAGES[i]
            pltpu.make_async_copy(
                my_rows(sendbuf, h, d0, dn, e), my_rows(routed, h, d0, dn, e), a_r.at[i]
            ).start()

            def send(k, carry):
                to = (e + k) % ne
                remote(
                    my_rows(sendbuf, h, d0, dn, to),
                    my_rows(routed, h, d0, dn, e),
                    a_s.at[i],
                    a_r.at[i],
                    (f, to),
                ).start()
                return carry

            lax.fori_loop(1, ne, send, 0)

    def arrived(i):
        h, d0, dn = STAGES[i]
        drain(routed.at[h, pl.ds(d0, dn)], a_r.at[i])

    pltpu.make_async_copy(wrows(wsend, e), wrows(wbuf, e), a_r.at[WSTAGE]).start()

    def send_weight(k, carry):
        to = (e + k) % ne
        remote(
            wrows(wsend, to), wrows(wbuf, e), a_s.at[WSTAGE], a_r.at[WSTAGE], (f, to)
        ).start()
        return carry

    lax.fori_loop(1, ne, send_weight, 0)
    exchange(0, len(STAGES))

    own_hid.wait()

    def activate(i, carry):
        rows = pl.ds(pl.multiple_of(i * 16, 16), 16)
        gate = hidv[rows, 0:1024].astype(F32)
        up = hidv[rows, 1024:2048].astype(F32)
        sigma = jax.nn.sigmoid(gate)
        silu = gate * sigma
        act[rows, :] = (silu * up).astype(BF16)
        bvec[rows, 0:1024] = up * sigma * (1.0 + gate * (1.0 - sigma))
        bvec[rows, 1024:2048] = silu
        return carry

    lax.fori_loop(0, 16, activate, 0)
    for d in (2, 1, 3):
        remote(
            act.at[pl.ds(0, 256)],
            act.at[pl.ds((4 - d) * 256, 256)],
            act_s.at[d],
            act_r.at[4 - d],
            at_x(d),
        ).start()

    drain(wq.at[:, pl.ds(128, 128), :], w_r.at[1])
    remote(
        wq.at[:, pl.ds(128, 128), :], wq.at[:, pl.ds(384, 128), :], w_s.at[2], w_r.at[3], sibling
    ).start()
    drain(wbuf, a_r.at[WSTAGE])
    own_w.wait()
    drain(wq.at[:, pl.ds(256, 128), :], w_r.at[2])
    drain(wq.at[:, pl.ds(384, 128), :], w_r.at[3])

    def scale(h, d):
        wcol = wbuf[:, d : d + 1].astype(F32)
        for b in range(4):
            part = routed[h, d, :, b * 128 : b * 128 + 128].astype(F32) * wcol
            sct[h, b * 128 : b * 128 + 128, d * 256 : d * 256 + 256] = part.T.astype(BF16)

    def back_part(h, d, n):
        cols = pl.ds(pl.multiple_of(n * 256, 256), 256)
        return jnp.dot(routed[h, d], wq[h, :, cols], preferred_element_type=F32), cols

    def grad_down_part(h):
        def sib(n, carry):
            cols = pl.ds(pl.multiple_of(n * 256, 256), 256)
            csend[h, :, cols] = jnp.dot(
                sct[h, 256:512, :], act[:, cols], preferred_element_type=F32
            ).astype(BF16)
            return carry

        lax.fori_loop(0, 4, sib, 0)
        remote(csend.at[h], crecv.at[h], c_s.at[h], c_r.at[h], sibling).start()

        def own(n, carry):
            cols = pl.ds(pl.multiple_of(n * 256, 256), 256)
            pown[h, :, cols] = jnp.dot(sct[h, 0:256, :], act[:, cols], preferred_element_type=F32)
            return carry

        lax.fori_loop(0, 4, own, 0)

    def over_z(h):
        drain(crecv.at[h], c_r.at[h])

        def add(n, carry):
            rows = pl.ds(pl.multiple_of(n * 16, 16), 16)
            rows2 = pl.ds(pl.multiple_of(128 + n * 16, 16), 16)
            zsend[h, rows, :] = (pown[h, rows2, :] + crecv[h, rows2, :].astype(F32)).astype(BF16)
            return carry

        lax.fori_loop(0, 8, add, 0)
        remote(zsend.at[h], zrecv.at[h], z_s.at[h], z_r.at[h], z_peer).start()

    for d in (1, 2, 3):
        drain(act.at[pl.ds(d * 256, 256)], act_r.at[d])
    arrived(0)
    for d in range(4):
        scale(0, d)
    grad_down_part(0)
    for d in range(4):

        def back0(n, carry, d=d):
            part, cols = back_part(0, d, n)
            bp[d, :, cols] = part
            return carry

        lax.fori_loop(0, 4, back0, 0)
        if d == 0:
            over_z(0)

    for i in range(1, len(STAGES)):
        d = STAGES[i][1]
        arrived(i)
        scale(1, d)
        if d:

            def back1(n, carry, d=d):
                part, cols = back_part(1, d, n)
                bsend[d - 1, :, cols] = (bp[d, :, cols] + part).astype(BF16)
                return carry

            lax.fori_loop(0, 4, back1, 0)
            remote(
                bsend.at[d - 1], brecv.at[3 - d], b_s.at[d - 1], b_r.at[3 - d], at_x(d)
            ).start()
    grad_down_part(1)

    def back_own(n, carry):
        part, cols = back_part(1, 0, n)
        bp[0, :, cols] = bp[0, :, cols] + part
        return carry

    lax.fori_loop(0, 4, back_own, 0)
    over_z(1)

    for d in range(3):
        drain(brecv.at[d], b_r.at[d])

    def finish(i, carry):
        rows = pl.ds(pl.multiple_of(i * 16, 16), 16)
        back = bp[0, rows, :] + brecv[0, rows, :].astype(F32)
        back = back + brecv[1, rows, :].astype(F32) + brecv[2, rows, :].astype(F32)
        slot_grad = jnp.sum(act[rows, :].astype(F32) * back, axis=1, keepdims=True)
        sgb[rows, :] = jnp.broadcast_to(slot_grad, (16, 128))
        hidden = wbuf[rows, 0:1].astype(F32) * back
        gp_out[rows, 0:1024] = (hidden * bvec[rows, 0:1024]).astype(BF16)
        gp_out[rows, 1024:2048] = (hidden * bvec[rows, 1024:2048]).astype(BF16)
        return carry

    lax.fori_loop(0, 16, finish, 0)

    pltpu.make_async_copy(wrows(sgb, e), wrows(ret, e), ret_r).start()

    def send_back(k, carry):
        to = (e + k) % ne
        remote(wrows(sgb, to), wrows(ret, e), ret_s, ret_r, (f, to)).start()
        return carry

    lax.fori_loop(1, ne, send_back, 0)

    for h in range(2):
        drain(zrecv.at[h], z_r.at[h])

        def total(n, carry):
            rows = pl.ds(pl.multiple_of(n * 16, 16), 16)
            mine = pown[h, rows, :] + crecv[h, rows, :].astype(F32)
            gd_out[pl.ds(pl.multiple_of(h * 128 + n * 16, 16), 16), :] = mine + zrecv[
                h, rows, :
            ].astype(F32)
            return carry

        lax.fori_loop(0, 8, total, 0)

    drain(ret, ret_r)
    per_slot = (gbuf[0].astype(F32) * ret[...]).reshape(ne, CAP, 128)
    per_expert = jnp.sum(per_slot, axis=1)
    ids8 = meta[0, 0:8, :]
    dp = jnp.zeros((8, 128), F32)
    for k in range(ne):
        dp = dp + jnp.where(ids8 == float(k), per_expert[k : k + 1, :], 0.0)
    dp_out[...] = dp

    for d in (1, 2, 3):
        drain(meta.at[0], meta_s.at[d])
        drain(ogb.at[0], og_s.at[d])
        drain(act.at[pl.ds(0, 256)], act_s.at[d])
        drain(bsend.at[0], b_s.at[d - 1])
    for i in range(3):
        drain(wq.at[:, pl.ds(0, 128), :], w_s.at[i])
    for h in range(2):
        drain(csend.at[h], c_s.at[h])
        drain(zsend.at[h], z_s.at[h])
    for i, (h, d0, dn) in enumerate(STAGES):
        drain(sendbuf.at[h, pl.ds(d0, dn), pl.ds(0, (ne - 1) * CAP), :], a_s.at[i])
    drain(wsend.at[pl.ds(0, (ne - 1) * CAP)], a_s.at[WSTAGE])
    drain(sgb.at[pl.ds(0, (ne - 1) * CAP)], ret_s)


def per_device(out_grad, router_probs, expert_ids, saved_hidden, w_down):
    dma = pltpu.SemaphoreType.DMA
    vmem = pl.BlockSpec(memory_space=pltpu.VMEM)
    hbm = pl.BlockSpec(memory_space=pl.ANY)
    stages = len(STAGES) + 1
    dp, gp, gd = pl.pallas_call(
        kernel,
        out_shape=(
            jax.ShapeDtypeStruct((8, 128), F32),
            jax.ShapeDtypeStruct((256, 2048), BF16),
            jax.ShapeDtypeStruct((256, 1024), F32),
        ),
        in_specs=[vmem, vmem, hbm, hbm, hbm],
        out_specs=(vmem, vmem, vmem),
        scratch_shapes=[
            pltpu.VMEM((4, 16, 128), F32),
            pltpu.VMEM((4, 4, 128, 256), BF16),
            pltpu.VMEM((4, 256, 128), BF16),
            pltpu.VMEM((256, 128), BF16),
            pltpu.VMEM((256, 128), BF16),
            pltpu.VMEM((2, 4, 256, 512), BF16),
            pltpu.VMEM((2, 4, 256, 512), BF16),
            pltpu.VMEM((256, 2048), BF16),
            pltpu.VMEM((1024, 1024), BF16),
            pltpu.VMEM((256, 2048), F32),
            pltpu.VMEM((2, 512, 1024), BF16),
            pltpu.VMEM((2, 512, 1024), BF16),
            pltpu.VMEM((2, 256, 1024), F32),
            pltpu.VMEM((2, 256, 1024), BF16),
            pltpu.VMEM((2, 256, 1024), BF16),
            pltpu.VMEM((2, 128, 1024), BF16),
            pltpu.VMEM((2, 128, 1024), BF16),
            pltpu.VMEM((4, 256, 1024), F32),
            pltpu.VMEM((3, 256, 1024), BF16),
            pltpu.VMEM((3, 256, 1024), BF16),
            pltpu.VMEM((256, 128), F32),
            pltpu.VMEM((256, 128), F32),
            dma,
            dma((4,)), dma((4,)),
            dma((4,)), dma((4,)),
            dma((3,)), dma((4,)),
            dma((4,)), dma((4,)),
            dma((stages,)), dma((stages,)),
            dma((2,)), dma((2,)),
            dma((2,)), dma((2,)),
            dma((3,)), dma((3,)),
            dma, dma,
        ],
        compiler_params=pltpu.CompilerParams(
            collective_id=0, has_side_effects=True, vmem_limit_bytes=56 * 2**20
        ),
    )(
        expert_ids.T,
        router_probs.T,
        out_grad,
        saved_hidden.reshape(256, 2048),
        w_down.reshape(2, 128, 1024),
    )
    return dp.T, gp.reshape(1, 1, 256, 2048), gd.reshape(1, 256, 1024)


def solution(mesh):
    placed = (
        P(("fsdp", "expert"), None),
        P(("fsdp", "expert"), None),
        P(("fsdp", "expert"), None),
        P("fsdp", "expert", None, None),
        P("expert", "fsdp", None),
    )
    return jax.shard_map(
        per_device,
        mesh=mesh,
        in_specs=placed,
        out_specs=(
            P(("fsdp", "expert"), None),
            P("fsdp", "expert", None, None),
            P("expert", "fsdp", None),
        ),
        check_vma=False,
    )
```

time: 378 us -> 130 us (0.34)
  waiting for transfers between devices: 288 us -> 0 us
  Pallas kernels: 0 us -> 125 us
  starting transfers between devices: 23.7 us -> 0 us
  local copies, waits for them, and re-layouts: 24.6 us -> 4.62 us
  matrix products: 17.3 us -> 0 us
  between operations: 14.3 us -> 0.65 us
  other arithmetic: 9.38 us -> 0 us
    reduce_scatter x1 -> x0, waiting for transfers between devices: 193 us -> none  [per_device(): lax.psum_scatter(lax.dot_general(scaled, activation, (((0,), (0,)), ((),...]
    pallas_call x0 -> x1, Pallas kernels: none -> 125 us  [per_device(): pl.pallas_call(kernel, out_shape=(jax.ShapeDtypeStruct((8, 128), F32), ja...]
    all_to_all x3 -> x0, waiting for transfers between devices: 94.1 us -> none  [the longest x1 86.1 us: per_device(): lax.all_to_all(send_rows, 'expert', split_axis=0, concat_axis=0, tiled=True)]
    all_to_all x3 -> x0, starting transfers between devices: 23.6 us -> none  [the longest x1 10.7 us: per_device(): lax.all_to_all(slot_grad.reshape(experts, CAP), 'expert', split_axis=0, c...]
    dot_general x2 -> x0, matrix products: 17.3 us -> none  [the longest x1 9.76 us: per_device(): lax.dot_general(scaled, activation, (((0,), (0,)), ((), ())), preferred_e...]
    gather x4 -> x0, local copies, waits for them, and re-layouts: 10.7 us -> none  [the longest x2 6.91 us: per_device(): returned[safe]]
    scatter x2 -> x0, local copies, waits for them, and re-layouts: 8.61 us -> none  [the longest x1 4.3 us: route_block(): filled = jnp.zeros((experts * capacity,), jnp.int32).at[slot_of].set(jnp....]
    another operation x3 -> x0, other arithmetic: 4.63 us -> none
  transfers between devices with their start and end apart: 5 -> 0, of which waited for: 4 -> 0; matrix products, arithmetic and copies ran while one was open for 13% -> 0% of each run, Pallas kernels for 0% -> 0%
where the time goes in v1:
time: 130 us
  Pallas kernels  125 us (96%)
  local copies, waits for them, and re-layouts  4.62 us (4%)
    pallas_call x1, Pallas kernels, per_device(): pl.pallas_call(kernel, out_shape=(jax.ShapeDtypeStruct((8, 128), F32), ja...  125 us
    unnamed x7, local copies, waits for them, and re-layouts  4.62 us

profile of v1, /device:TPU:1, one launch (start us, length us, event | category | flops | bytes accessed | tf_op | source)
XLA Modules:
  0.0 130.0 jit_solution(1192525401297105237)
XLA Ops:
  0.6 124.7 %shard_map.76 = (f32[8,128]{1,0:T(8,128)}, bf16[256,2048]{1,0:T(8,128)(2,1)}, f32[256,1024]{1,0:T(8,128)}) custom-call(s32[8,128]{1,0:T(8,128)} %bitcast.11, bf16[8,128]{1,0:T(8,128)(2,1)} %bitcast.13, bf16[128,4096]{1,0:T(8,128)(2,1)} %og_hbm.1, bf16[256,2048]{1,0:T(8,128)(2,1)} %bitcast.7, bf16[2,128,1024]{2,1,0:T(8,128)(2,1)} %bitcast.10), custom_call_target="tpu_custom_call" | custom-call | tf_op jit(solution)/shard_map/pallas_call | solution.py:340
  125.3 0.0 copy-start.1
  125.3 0.7 copy-done.1
  126.0 0.6 copy.11
  126.6 0.0 copy-start
  126.6 2.4 %copy.12 = bf16[1,1,256,2048]{3,2,1,0:T(8,128)(2,1)} copy(bf16[1,1,256,2048]{3,2,1,0:T(8,128)(2,1)} %bitcast.9) | data formatting | bytes 2097152
  129.0 0.0 copy-done
  129.0 1.0 copy.13
Async XLA Ops:
  125.3 0.7 copy-start.1
  126.6 2.4 %copy-start = (f32[256,1024]{1,0:T(8,128)S(1)}, f32[256,1024]{1,0:T(8,128)}, u32[]{:S(2)}) copy-start(f32[256,1024]{1,0:T(8,128)} %get-tuple-element.8) | copy-start | bytes 3145732

commit v2 on v1

--- a/solution.py
+++ b/solution.py
@@ -12,14 +12,17 @@
 NX = 4
 STAGES = ((0, 0, 4), (1, 2, 1), (1, 1, 1), (1, 3, 1), (1, 0, 1))
 WSTAGE = len(STAGES)
+ZAT = (4, 4)
+ZPARTS = len(ZAT)
+ZROWS = 256 // ZPARTS
 
 
 def kernel(
-    ids_ref, probs_ref, og_hbm, hid_hbm, w_hbm,
+    ids_hbm, probs_hbm, og_hbm, hid_hbm, w_hbm,
     dp_out, gp_out, gd_out,
     meta, ogb, gbuf, wsend, wbuf, sendbuf, routed, hidv, act, bvec, wq, sct, pown,
     csend, crecv, zsend, zrecv, bp, bsend, brecv, sgb, ret,
-    hid_sem, meta_s, meta_r, og_s, og_r, w_s, w_r, act_s, act_r, a_s, a_r,
+    ids_ref, probs_ref, in_sem, hid_sem, meta_s, meta_r, og_s, og_r, w_s, w_r, act_s, act_r, a_s, a_r,
     c_s, c_r, z_s, z_r, b_s, b_r, ret_s, ret_r,
 ):
     ne = 16
@@ -41,20 +44,12 @@
     def drain(ref, sem):
         pltpu.make_async_copy(ref, ref, sem).wait()
 
-    own_w = pltpu.make_async_copy(w_hbm, wq.at[:, pl.ds(0, 128), :], w_r.at[0])
+    own_w = pltpu.make_async_copy(w_hbm, wq.at[1, pl.ds(0, 256), :], w_r.at[0])
     own_hid = pltpu.make_async_copy(hid_hbm, hidv, hid_sem)
 
-    def og_columns(xt, b):
-        dz, dc = b % 2, b // 2
-        col = ((zh + dz) % 2) * 2048 + xt * 512 + ((c + dc) % 2) * 256
-        return og_hbm.at[:, pl.ds(pl.multiple_of(col, 256), 256)]
-
-    for b in range(4):
-        pltpu.make_async_copy(og_columns(x, b), ogb.at[0, b], og_r.at[0]).start()
-    own_hid.start()
-    own_w.start()
-    meta[0, 0:8, :] = ids_ref[...].astype(F32)
-    meta[0, 8:16, :] = probs_ref[...].astype(F32)
+    def og_columns(xt, h):
+        col = ((zh + 1 - h) % 2) * 2048 + xt * 512
+        return og_hbm.at[:, pl.ds(pl.multiple_of(col, 512), 512)]
 
     barrier = pltpu.get_barrier_semaphore()
     for d in (1, 2, 3):
@@ -67,17 +62,34 @@
         return carry
 
     lax.fori_loop(1, ne, greet, 0)
+    for h in range(2):
+        pltpu.make_async_copy(og_columns(x, h), ogb.at[0, h], og_r.at[h, 0]).start()
+    own_hid.start()
+    own_w.start()
+    own_ids = pltpu.make_async_copy(ids_hbm, ids_ref, in_sem.at[0])
+    own_probs = pltpu.make_async_copy(probs_hbm, probs_ref, in_sem.at[1])
+    own_ids.start()
+    own_probs.start()
+    own_ids.wait()
+    own_probs.wait()
+    meta[0, 0:8, :] = ids_ref[...].astype(F32)
+    meta[0, 8:16, :] = probs_ref[...].astype(F32)
     pl.semaphore_wait(barrier, 5 + ne - 1)
 
     for d in (2, 1, 3):
         remote(meta.at[0], meta.at[4 - d], meta_s.at[d], meta_r.at[4 - d], at_x(d)).start()
-    for d in (2, 1, 3):
-        for b in range(4):
+    for h in range(2):
+        for d in (2, 1, 3):
             remote(
-                og_columns((x + d) % 4, b), ogb.at[4 - d, b], og_s.at[d], og_r.at[4 - d], at_x(d)
+                og_columns((x + d) % 4, h),
+                ogb.at[4 - d, h],
+                og_s.at[h, d],
+                og_r.at[h, 4 - d],
+                at_x(d),
             ).start()
-    remote(w_hbm, wq.at[:, pl.ds(128, 128), :], w_s.at[0], w_r.at[1], z_peer).start()
-    remote(w_hbm, wq.at[:, pl.ds(256, 128), :], w_s.at[1], w_r.at[2], sibling).start()
+        if h == 0:
+            remote(w_hbm, wq.at[0, pl.ds(0, 256), :], w_s.at[0], w_r.at[1], z_peer).start()
+            remote(w_hbm, wq.at[1, pl.ds(256, 256), :], w_s.at[1], w_r.at[2], sibling).start()
 
     tri_r = lax.broadcasted_iota(jnp.int32, (128, 128), 0)
     tri_c = lax.broadcasted_iota(jnp.int32, (128, 128), 1)
@@ -105,13 +117,14 @@
         gbuf[d] = pick.reshape(ne * CAP, 128).astype(BF16)
     wsend[...] = wacc.astype(BF16)
 
-    for d in (0, 1, 3, 2):
-        drain(ogb.at[d], og_r.at[d])
-        g = gbuf[d]
-        for b in range(4):
-            rows = jnp.dot(g, ogb[d, b], preferred_element_type=F32).astype(BF16)
-            sendbuf[0, d, :, b * 128 : b * 128 + 128] = rows[:, :128]
-            sendbuf[1, d, :, b * 128 : b * 128 + 128] = rows[:, 128:]
+    def expand(h):
+        for d in (0, 1, 3, 2):
+            drain(ogb.at[d, h], og_r.at[h, d])
+            for dc in range(2):
+                columns = pl.ds(pl.multiple_of(((c + dc) % 2) * 256, 256), 256)
+                sendbuf[h, d, :, dc * 256 : dc * 256 + 256] = jnp.dot(
+                    gbuf[d], ogb[d, h, :, columns], preferred_element_type=F32
+                ).astype(BF16)
 
     def my_rows(ref, h, d0, dn, who):
         return ref.at[h, pl.ds(d0, dn), pl.ds(pl.multiple_of(who * CAP, CAP), CAP), :]
@@ -153,7 +166,10 @@
         return carry
 
     lax.fori_loop(1, ne, send_weight, 0)
-    exchange(0, len(STAGES))
+    expand(0)
+    exchange(0, 1)
+    expand(1)
+    exchange(1, 1)
 
     own_hid.wait()
 
@@ -178,14 +194,14 @@
             at_x(d),
         ).start()
 
-    drain(wq.at[:, pl.ds(128, 128), :], w_r.at[1])
+    drain(wq.at[0, pl.ds(0, 256), :], w_r.at[1])
     remote(
-        wq.at[:, pl.ds(128, 128), :], wq.at[:, pl.ds(384, 128), :], w_s.at[2], w_r.at[3], sibling
+        wq.at[0, pl.ds(0, 256), :], wq.at[0, pl.ds(256, 256), :], w_s.at[2], w_r.at[3], sibling
     ).start()
     drain(wbuf, a_r.at[WSTAGE])
     own_w.wait()
-    drain(wq.at[:, pl.ds(256, 128), :], w_r.at[2])
-    drain(wq.at[:, pl.ds(384, 128), :], w_r.at[3])
+    drain(wq.at[1, pl.ds(256, 256), :], w_r.at[2])
+    drain(wq.at[0, pl.ds(256, 256), :], w_r.at[3])
 
     def scale(h, d):
         wcol = wbuf[:, d : d + 1].astype(F32)
@@ -215,21 +231,20 @@
 
         lax.fori_loop(0, 4, own, 0)
 
-    def over_z(h):
-        drain(crecv.at[h], c_r.at[h])
+    def chip_sum():
+        drain(crecv.at[0], c_r.at[0])
 
         def add(n, carry):
             rows = pl.ds(pl.multiple_of(n * 16, 16), 16)
-            rows2 = pl.ds(pl.multiple_of(128 + n * 16, 16), 16)
-            zsend[h, rows, :] = (pown[h, rows2, :] + crecv[h, rows2, :].astype(F32)).astype(BF16)
+            zsend[rows, :] = (pown[0, rows, :] + crecv[0, rows, :].astype(F32)).astype(BF16)
             return carry
 
-        lax.fori_loop(0, 8, add, 0)
-        remote(zsend.at[h], zrecv.at[h], z_s.at[h], z_r.at[h], z_peer).start()
+        lax.fori_loop(0, 16, add, 0)
 
     for d in (1, 2, 3):
         drain(act.at[pl.ds(d * 256, 256)], act_r.at[d])
     arrived(0)
+    exchange(2, 1)
     for d in range(4):
         scale(0, d)
     grad_down_part(0)
@@ -242,11 +257,17 @@
 
         lax.fori_loop(0, 4, back0, 0)
         if d == 0:
-            over_z(0)
+            chip_sum()
 
     for i in range(1, len(STAGES)):
         d = STAGES[i][1]
         arrived(i)
+        if i + 2 < len(STAGES):
+            exchange(i + 2, 1)
+        for p in range(ZPARTS):
+            if i == ZAT[p]:
+                part = pl.ds(p * ZROWS, ZROWS)
+                remote(zsend.at[part], zrecv.at[part], z_s.at[p], z_r.at[p], z_peer).start()
         scale(1, d)
         if d:
 
@@ -267,7 +288,6 @@
         return carry
 
     lax.fori_loop(0, 4, back_own, 0)
-    over_z(1)
 
     for d in range(3):
         drain(brecv.at[d], b_r.at[d])
@@ -278,9 +298,7 @@
         back = back + brecv[1, rows, :].astype(F32) + brecv[2, rows, :].astype(F32)
         slot_grad = jnp.sum(act[rows, :].astype(F32) * back, axis=1, keepdims=True)
         sgb[rows, :] = jnp.broadcast_to(slot_grad, (16, 128))
-        hidden = wbuf[rows, 0:1].astype(F32) * back
-        gp_out[rows, 0:1024] = (hidden * bvec[rows, 0:1024]).astype(BF16)
-        gp_out[rows, 1024:2048] = (hidden * bvec[rows, 1024:2048]).astype(BF16)
+        bp[0, rows, :] = wbuf[rows, 0:1].astype(F32) * back
         return carry
 
     lax.fori_loop(0, 16, finish, 0)
@@ -294,18 +312,29 @@
 
     lax.fori_loop(1, ne, send_back, 0)
 
-    for h in range(2):
-        drain(zrecv.at[h], z_r.at[h])
-
-        def total(n, carry):
-            rows = pl.ds(pl.multiple_of(n * 16, 16), 16)
-            mine = pown[h, rows, :] + crecv[h, rows, :].astype(F32)
-            gd_out[pl.ds(pl.multiple_of(h * 128 + n * 16, 16), 16), :] = mine + zrecv[
-                h, rows, :
-            ].astype(F32)
-            return carry
-
-        lax.fori_loop(0, 8, total, 0)
+    def grad_pre(i, carry):
+        rows = pl.ds(pl.multiple_of(i * 16, 16), 16)
+        hidden = bp[0, rows, :]
+        gp_out[rows, 0:1024] = (hidden * bvec[rows, 0:1024]).astype(BF16)
+        gp_out[rows, 1024:2048] = (hidden * bvec[rows, 1024:2048]).astype(BF16)
+        return carry
+
+    lax.fori_loop(0, 16, grad_pre, 0)
+
+    drain(crecv.at[1], c_r.at[1])
+
+    def chip_total(n, carry):
+        rows = pl.ds(pl.multiple_of(n * 16, 16), 16)
+        pown[1, rows, :] = pown[1, rows, :] + crecv[1, rows, :].astype(F32)
+        return carry
+
+    lax.fori_loop(0, 16, chip_total, 0)
+
+    def total(n, carry):
+        rows = pl.ds(pl.multiple_of(n * 16, 16), 16)
+        gd_out[rows, :] = pown[1, rows, :] + zrecv[rows, :].astype(F32)
+        return carry
+
 
     drain(ret, ret_r)
     per_slot = (gbuf[0].astype(F32) * ret[...]).reshape(ne, CAP, 128)
@@ -316,20 +345,37 @@
         dp = dp + jnp.where(ids8 == float(k), per_expert[k : k + 1, :], 0.0)
     dp_out[...] = dp
 
+    for p in range(ZPARTS):
+        drain(zrecv.at[pl.ds(p * ZROWS, ZROWS)], z_r.at[p])
+        lax.fori_loop(p * ZROWS // 16, (p + 1) * ZROWS // 16, total, 0)
+
     for d in (1, 2, 3):
         drain(meta.at[0], meta_s.at[d])
-        drain(ogb.at[0], og_s.at[d])
+        for h in range(2):
+            drain(ogb.at[0, h], og_s.at[h, d])
         drain(act.at[pl.ds(0, 256)], act_s.at[d])
         drain(bsend.at[0], b_s.at[d - 1])
     for i in range(3):
-        drain(wq.at[:, pl.ds(0, 128), :], w_s.at[i])
+        drain(wq.at[0, pl.ds(0, 256), :], w_s.at[i])
     for h in range(2):
         drain(csend.at[h], c_s.at[h])
-        drain(zsend.at[h], z_s.at[h])
+    for p in range(ZPARTS):
+        drain(zsend.at[pl.ds(p * ZROWS, ZROWS)], z_s.at[p])
     for i, (h, d0, dn) in enumerate(STAGES):
         drain(sendbuf.at[h, pl.ds(d0, dn), pl.ds(0, (ne - 1) * CAP), :], a_s.at[i])
     drain(wsend.at[pl.ds(0, (ne - 1) * CAP)], a_s.at[WSTAGE])
     drain(sgb.at[pl.ds(0, (ne - 1) * CAP)], ret_s)
+
+
+def write_out(dp, gp, gd, dp_out, gp_out, gd_out, sem):
+    copies = [
+        pltpu.make_async_copy(src, dst, sem.at[i])
+        for i, (src, dst) in enumerate(((gp, gp_out), (gd, gd_out), (dp, dp_out)))
+    ]
+    for copy in copies:
+        copy.start()
+    for copy in copies:
+        copy.wait()
 
 
 def per_device(out_grad, router_probs, expert_ids, saved_hidden, w_down):
@@ -340,15 +386,15 @@
     dp, gp, gd = pl.pallas_call(
         kernel,
         out_shape=(
-            jax.ShapeDtypeStruct((8, 128), F32),
-            jax.ShapeDtypeStruct((256, 2048), BF16),
-            jax.ShapeDtypeStruct((256, 1024), F32),
+            pltpu.VMEM((8, 128), F32),
+            pltpu.VMEM((256, 2048), BF16),
+            pltpu.VMEM((256, 1024), F32),
         ),
-        in_specs=[vmem, vmem, hbm, hbm, hbm],
+        in_specs=[hbm] * 5,
         out_specs=(vmem, vmem, vmem),
         scratch_shapes=[
             pltpu.VMEM((4, 16, 128), F32),
-            pltpu.VMEM((4, 4, 128, 256), BF16),
+            pltpu.VMEM((4, 2, 128, 512), BF16),
             pltpu.VMEM((4, 256, 128), BF16),
             pltpu.VMEM((256, 128), BF16),
             pltpu.VMEM((256, 128), BF16),
@@ -362,21 +408,24 @@
             pltpu.VMEM((2, 256, 1024), F32),
             pltpu.VMEM((2, 256, 1024), BF16),
             pltpu.VMEM((2, 256, 1024), BF16),
-            pltpu.VMEM((2, 128, 1024), BF16),
-            pltpu.VMEM((2, 128, 1024), BF16),
+            pltpu.VMEM((256, 1024), BF16),
+            pltpu.VMEM((256, 1024), BF16),
             pltpu.VMEM((4, 256, 1024), F32),
             pltpu.VMEM((3, 256, 1024), BF16),
             pltpu.VMEM((3, 256, 1024), BF16),
             pltpu.VMEM((256, 128), F32),
             pltpu.VMEM((256, 128), F32),
+            pltpu.VMEM((8, 128), jnp.int32),
+            pltpu.VMEM((8, 128), BF16),
+            dma((2,)),
             dma,
             dma((4,)), dma((4,)),
-            dma((4,)), dma((4,)),
+            dma((2, 4)), dma((2, 4)),
             dma((3,)), dma((4,)),
             dma((4,)), dma((4,)),
             dma((stages,)), dma((stages,)),
             dma((2,)), dma((2,)),
-            dma((2,)), dma((2,)),
+            dma((ZPARTS,)), dma((ZPARTS,)),
             dma((3,)), dma((3,)),
             dma, dma,
         ],
@@ -388,8 +437,19 @@
         router_probs.T,
         out_grad,
         saved_hidden.reshape(256, 2048),
-        w_down.reshape(2, 128, 1024),
+        w_down.reshape(256, 1024),
     )
+    dp, gp, gd = pl.pallas_call(
+        write_out,
+        out_shape=(
+            jax.ShapeDtypeStruct((8, 128), F32),
+            jax.ShapeDtypeStruct((256, 2048), BF16),
+            jax.ShapeDtypeStruct((256, 1024), F32),
+        ),
+        in_specs=[hbm] * 3,
+        out_specs=(hbm,) * 3,
+        scratch_shapes=[dma((3,))],
+    )(*(pltpu.with_memory_space_constraint(v, pltpu.VMEM) for v in (dp, gp, gd)))
     return dp.T, gp.reshape(1, 1, 256, 2048), gd.reshape(1, 256, 1024)
 
 

time: 130 us -> 112 us (0.86)
  Pallas kernels: 125 us -> 112 us
  local copies, waits for them, and re-layouts: 4.62 us -> 0 us
    pallas_call x1 -> x2, Pallas kernels: 125 us -> 112 us  [the longest x1 110 us: per_device(): pl.pallas_call(kernel, out_shape=(pltpu.VMEM((8, 128), F32), pltpu.VMEM((...]
    unnamed x7 -> x0, local copies, waits for them, and re-layouts: 4.62 us -> none
where the time goes in v2:
time: 112 us
  Pallas kernels  112 us (100%)
    pallas_call x1, Pallas kernels, per_device(): pl.pallas_call(kernel, out_shape=(pltpu.VMEM((8, 128), F32), pltpu.VMEM((...  110 us

profile of v2, /device:TPU:1, one launch (start us, length us, event | category | flops | bytes accessed | tf_op | source)
XLA Modules:
  0.0 112.3 jit_solution(1520374241910422806)
XLA Ops:
  0.6 110.3 %shard_map.76 = (f32[8,128]{1,0:T(8,128)S(1)}, bf16[256,2048]{1,0:T(8,128)(2,1)S(1)}, f32[256,1024]{1,0:T(8,128)S(1)}) custom-call(s32[8,128]{1,0:T(8,128)} %bitcast.9, bf16[8,128]{1,0:T(8,128)(2,1)} %bitcast.10, bf16[128,4096]{1,0:T(8,128)(2,1)} %og_hbm.1, bf16[256,2048]{1,0:T(8,128)(2,1)} %bitcast.7, bf16[256,1024]{1,0:T(8,128)(2,1)} %bitcast.8), custom_call_target="tpu_custom_call" | custom-call | tf_op jit(solution)/shard_map/pallas_call | solution.py:386
  111.0 1.3 %shard_map.77 = (f32[8,128]{1,0:T(8,128)}, bf16[256,2048]{1,0:T(8,128)(2,1)}, f32[256,1024]{1,0:T(8,128)}) custom-call(f32[8,128]{1,0:T(8,128)S(1)} %get-tuple-element.9.dp, bf16[256,2048]{1,0:T(8,128)(2,1)S(1)} %get-tuple-element.10.gp, f32[256,1024]{1,0:T(8,128)S(1)} %get-tuple-element.11.gd), custom_call_target="tpu_custom_call" | custom-call | tf_op jit(solution)/shard_map/pallas_call | solution.py:442

commit v3 on v2

--- a/solution.py
+++ b/solution.py
@@ -10,10 +10,11 @@
 MESH = pl.DeviceIdType.MESH
 CAP = 16
 NX = 4
-STAGES = ((0, 0, 4), (1, 2, 1), (1, 1, 1), (1, 3, 1), (1, 0, 1))
+STAGES = ((0, 1, 3), (1, 2, 1), (1, 1, 1), (1, 3, 1), (0, 0, 1), (1, 0, 1))
 WSTAGE = len(STAGES)
-ZAT = (4, 4)
-ZPARTS = len(ZAT)
+ISSUE = ((1, 5), (6, 0), (6, 0))
+ZPARTS = 8
+ZFIRST = 5
 ZROWS = 256 // ZPARTS
 
 
@@ -24,17 +25,36 @@
     csend, crecv, zsend, zrecv, bp, bsend, brecv, sgb, ret,
     ids_ref, probs_ref, in_sem, hid_sem, meta_s, meta_r, og_s, og_r, w_s, w_r, act_s, act_r, a_s, a_r,
     c_s, c_r, z_s, z_r, b_s, b_r, ret_s, ret_r,
+    acth, wswap, bgive, btake, as_s, as_r, ws_s, ws_r, bs_s, bs_r,
 ):
     ne = 16
     f = lax.axis_index("fsdp")
     e = lax.axis_index("expert")
     zh, x, c = f // 8, (f // 2) % 4, f % 2
+    zl, y = e // 4, e % 4
 
     def at_x(d):
         return (zh * 8 + ((x + d) % 4) * 2 + c, e)
 
     z_peer = ((1 - zh) * 8 + x * 2 + c, e)
     sibling = (zh * 8 + x * 2 + 1 - c, e)
+
+    def away(to):
+        gap = (zl - to // 4) * (zl - to // 4)
+        return gap // 9 + ((gap // 4) % 2) * ((y + to % 4) % 2)
+
+    def near(to):
+        return (((zh + away(to)) % 2) * 8 + x * 2 + c, to)
+
+    def for_away(do):
+        def one(to, carry):
+            @pl.when(away(to) == 1)
+            def _():
+                do(to)
+
+            return carry
+
+        lax.fori_loop(0, ne, one, 0)
 
     def remote(src, dst, ss, rs, dev):
         return pltpu.make_async_remote_copy(
@@ -58,10 +78,16 @@
     pl.semaphore_signal(barrier, inc=1, device_id=sibling, device_id_type=MESH)
 
     def greet(k, carry):
-        pl.semaphore_signal(barrier, inc=1, device_id=(f, (e + k) % ne), device_id_type=MESH)
-        return carry
-
-    lax.fori_loop(1, ne, greet, 0)
+        to = (e + k) % ne
+        pl.semaphore_signal(barrier, inc=1, device_id=near(to), device_id_type=MESH)
+
+        @pl.when(away(to) == 1)
+        def _():
+            pl.semaphore_signal(barrier, inc=1, device_id=(f, to), device_id_type=MESH)
+
+        return carry + away(to)
+
+    extra = lax.fori_loop(1, ne, greet, 0)
     for h in range(2):
         pltpu.make_async_copy(og_columns(x, h), ogb.at[0, h], og_r.at[h, 0]).start()
     own_hid.start()
@@ -74,7 +100,36 @@
     own_probs.wait()
     meta[0, 0:8, :] = ids_ref[...].astype(F32)
     meta[0, 8:16, :] = probs_ref[...].astype(F32)
-    pl.semaphore_wait(barrier, 5 + ne - 1)
+
+    own_hid.wait()
+
+    def wrows(ref, who):
+        return ref.at[pl.ds(pl.multiple_of(who * CAP, CAP), CAP), :]
+
+    def activate(i, carry):
+        rows = pl.ds(pl.multiple_of(i * CAP, CAP), CAP)
+        gate = hidv[rows, 0:1024].astype(F32)
+        up = hidv[rows, 1024:2048].astype(F32)
+        sigma = jax.nn.sigmoid(gate)
+        silu = gate * sigma
+        bvec[rows, 0:1024] = up * sigma * (1.0 + gate * (1.0 - sigma))
+        bvec[rows, 1024:2048] = silu
+        value = (silu * up).astype(BF16)
+        acth[rows, :] = value
+
+        @pl.when(away(i) == 0)
+        def _():
+            act[rows, :] = value
+
+        return carry
+
+    lax.fori_loop(0, ne, activate, 0)
+    pl.semaphore_wait(barrier, 5 + ne - 1 + extra)
+    for_away(
+        lambda to: remote(
+            wrows(acth, to), wrows(act, to), as_s.at[to], as_r.at[to], z_peer
+        ).start()
+    )
 
     for d in (2, 1, 3):
         remote(meta.at[0], meta.at[4 - d], meta_s.at[d], meta_r.at[4 - d], at_x(d)).start()
@@ -129,9 +184,6 @@
     def my_rows(ref, h, d0, dn, who):
         return ref.at[h, pl.ds(d0, dn), pl.ds(pl.multiple_of(who * CAP, CAP), CAP), :]
 
-    def wrows(ref, who):
-        return ref.at[pl.ds(pl.multiple_of(who * CAP, CAP), CAP), :]
-
     def exchange(first, count):
         for i in range(first, first + count):
             h, d0, dn = STAGES[i]
@@ -142,11 +194,11 @@
             def send(k, carry):
                 to = (e + k) % ne
                 remote(
-                    my_rows(sendbuf, h, d0, dn, to),
+                    my_rows(sendbuf, (h + away(to)) % 2, d0, dn, to),
                     my_rows(routed, h, d0, dn, e),
                     a_s.at[i],
                     a_r.at[i],
-                    (f, to),
+                    near(to),
                 ).start()
                 return carry
 
@@ -161,30 +213,17 @@
     def send_weight(k, carry):
         to = (e + k) % ne
         remote(
-            wrows(wsend, to), wrows(wbuf, e), a_s.at[WSTAGE], a_r.at[WSTAGE], (f, to)
+            wrows(wsend, to), wrows(wbuf, e), a_s.at[WSTAGE], a_r.at[WSTAGE], near(to)
         ).start()
         return carry
 
     lax.fori_loop(1, ne, send_weight, 0)
     expand(0)
+    expand(1)
     exchange(0, 1)
-    expand(1)
-    exchange(1, 1)
-
-    own_hid.wait()
-
-    def activate(i, carry):
-        rows = pl.ds(pl.multiple_of(i * 16, 16), 16)
-        gate = hidv[rows, 0:1024].astype(F32)
-        up = hidv[rows, 1024:2048].astype(F32)
-        sigma = jax.nn.sigmoid(gate)
-        silu = gate * sigma
-        act[rows, :] = (silu * up).astype(BF16)
-        bvec[rows, 0:1024] = up * sigma * (1.0 + gate * (1.0 - sigma))
-        bvec[rows, 1024:2048] = silu
-        return carry
-
-    lax.fori_loop(0, 16, activate, 0)
+    exchange(*ISSUE[0])
+
+    for_away(lambda to: drain(wrows(act, to), as_r.at[to]))
     for d in (2, 1, 3):
         remote(
             act.at[pl.ds(0, 256)],
@@ -199,6 +238,11 @@
         wq.at[0, pl.ds(0, 256), :], wq.at[0, pl.ds(256, 256), :], w_s.at[2], w_r.at[3], sibling
     ).start()
     drain(wbuf, a_r.at[WSTAGE])
+    for_away(
+        lambda to: remote(
+            wrows(wbuf, to), wrows(wswap, to), ws_s.at[to], ws_r.at[to], z_peer
+        ).start()
+    )
     own_w.wait()
     drain(wq.at[1, pl.ds(256, 256), :], w_r.at[2])
     drain(wq.at[0, pl.ds(256, 256), :], w_r.at[3])
@@ -241,67 +285,101 @@
 
         lax.fori_loop(0, 16, add, 0)
 
-    for d in (1, 2, 3):
-        drain(act.at[pl.ds(d * 256, 256)], act_r.at[d])
-    arrived(0)
-    exchange(2, 1)
-    for d in range(4):
-        scale(0, d)
-    grad_down_part(0)
-    for d in range(4):
-
-        def back0(n, carry, d=d):
+    def back_first(d):
+        def one(n, carry):
             part, cols = back_part(0, d, n)
             bp[d, :, cols] = part
             return carry
 
-        lax.fori_loop(0, 4, back0, 0)
-        if d == 0:
-            chip_sum()
-
-    for i in range(1, len(STAGES)):
-        d = STAGES[i][1]
-        arrived(i)
-        if i + 2 < len(STAGES):
-            exchange(i + 2, 1)
-        for p in range(ZPARTS):
-            if i == ZAT[p]:
-                part = pl.ds(p * ZROWS, ZROWS)
-                remote(zsend.at[part], zrecv.at[part], z_s.at[p], z_r.at[p], z_peer).start()
-        scale(1, d)
+        lax.fori_loop(0, 4, one, 0)
+
+    def back_second(d):
+        def one(n, carry):
+            part, cols = back_part(1, d, n)
+            if d:
+                bsend[d - 1, :, cols] = (bp[d, :, cols] + part).astype(BF16)
+            else:
+                bp[0, :, cols] = bp[0, :, cols] + part
+            return carry
+
+        lax.fori_loop(0, 4, one, 0)
         if d:
-
-            def back1(n, carry, d=d):
-                part, cols = back_part(1, d, n)
-                bsend[d - 1, :, cols] = (bp[d, :, cols] + part).astype(BF16)
-                return carry
-
-            lax.fori_loop(0, 4, back1, 0)
             remote(
                 bsend.at[d - 1], brecv.at[3 - d], b_s.at[d - 1], b_r.at[3 - d], at_x(d)
             ).start()
+
+    def start_z(p):
+        part = pl.ds(p * ZROWS, ZROWS)
+        remote(zsend.at[part], zrecv.at[part], z_s.at[p], z_r.at[p], z_peer).start()
+
+    arrived(0)
+    exchange(*ISSUE[1])
+    for d in (2, 1, 3):
+        back_first(d)
+    arrived(1)
+    exchange(*ISSUE[2])
+    back_second(2)
+    arrived(2)
+    back_second(1)
+    arrived(3)
+    back_second(3)
+    for d in (1, 2, 3):
+        drain(act.at[pl.ds(d * 256, 256)], act_r.at[d])
+    for d in (2, 1, 3):
+        scale(0, d)
+    arrived(4)
+    scale(0, 0)
+    grad_down_part(0)
+    for d in (2, 1, 3):
+        scale(1, d)
+    chip_sum()
+    arrived(5)
+    for p in range(ZFIRST):
+        start_z(p)
+    scale(1, 0)
     grad_down_part(1)
-
-    def back_own(n, carry):
-        part, cols = back_part(1, 0, n)
-        bp[0, :, cols] = bp[0, :, cols] + part
-        return carry
-
-    lax.fori_loop(0, 4, back_own, 0)
+    back_first(0)
+    back_second(0)
 
     for d in range(3):
         drain(brecv.at[d], b_r.at[d])
 
-    def finish(i, carry):
-        rows = pl.ds(pl.multiple_of(i * 16, 16), 16)
+    def sum_x(i, carry):
+        rows = pl.ds(pl.multiple_of(i * CAP, CAP), CAP)
         back = bp[0, rows, :] + brecv[0, rows, :].astype(F32)
         back = back + brecv[1, rows, :].astype(F32) + brecv[2, rows, :].astype(F32)
-        slot_grad = jnp.sum(act[rows, :].astype(F32) * back, axis=1, keepdims=True)
+        bp[0, rows, :] = back
+
+        @pl.when(away(i) == 1)
+        def _():
+            bgive[rows, :] = back.astype(BF16)
+            remote(
+                wrows(bgive, i), wrows(btake, i), bs_s.at[i], bs_r.at[i], z_peer
+            ).start()
+
+        return carry
+
+    lax.fori_loop(0, ne, sum_x, 0)
+    for p in range(ZFIRST, ZPARTS):
+        start_z(p)
+
+    def take(to):
+        rows = pl.ds(pl.multiple_of(to * CAP, CAP), CAP)
+        drain(wrows(btake, to), bs_r.at[to])
+        drain(wrows(wswap, to), ws_r.at[to])
+        bp[0, rows, :] = btake[rows, :].astype(F32)
+
+    def finish(i, carry):
+        rows = pl.ds(pl.multiple_of(i * CAP, CAP), CAP)
+        back = bp[0, rows, :]
+        slot_grad = jnp.sum(acth[rows, :].astype(F32) * back, axis=1, keepdims=True)
         sgb[rows, :] = jnp.broadcast_to(slot_grad, (16, 128))
-        bp[0, rows, :] = wbuf[rows, 0:1].astype(F32) * back
-        return carry
-
-    lax.fori_loop(0, 16, finish, 0)
+        weight = jnp.where(away(i) == 1, wswap[rows, 0:1].astype(F32), wbuf[rows, 0:1].astype(F32))
+        bp[0, rows, :] = weight * back
+        return carry
+
+    for_away(take)
+    lax.fori_loop(0, ne, finish, 0)
 
     pltpu.make_async_copy(wrows(sgb, e), wrows(ret, e), ret_r).start()
 
@@ -349,6 +427,12 @@
         drain(zrecv.at[pl.ds(p * ZROWS, ZROWS)], z_r.at[p])
         lax.fori_loop(p * ZROWS // 16, (p + 1) * ZROWS // 16, total, 0)
 
+    def left(to):
+        drain(wrows(acth, to), as_s.at[to])
+        drain(wrows(wbuf, to), ws_s.at[to])
+        drain(wrows(bgive, to), bs_s.at[to])
+
+    for_away(left)
     for d in (1, 2, 3):
         drain(meta.at[0], meta_s.at[d])
         for h in range(2):
@@ -428,6 +512,13 @@
             dma((ZPARTS,)), dma((ZPARTS,)),
             dma((3,)), dma((3,)),
             dma, dma,
+            pltpu.VMEM((256, 1024), BF16),
+            pltpu.VMEM((256, 128), BF16),
+            pltpu.VMEM((256, 1024), BF16),
+            pltpu.VMEM((256, 1024), BF16),
+            dma((16,)), dma((16,)),
+            dma((16,)), dma((16,)),
+            dma((16,)), dma((16,)),
         ],
         compiler_params=pltpu.CompilerParams(
             collective_id=0, has_side_effects=True, vmem_limit_bytes=56 * 2**20

time: 112 us -> 107 us (0.955)
  Pallas kernels: 112 us -> 107 us
    pallas_call x1, Pallas kernels: 110 us -> 105 us  [per_device(): pl.pallas_call(kernel, out_shape=(pltpu.VMEM((8, 128), F32), pltpu.VMEM((...]
where the time goes in v3:
time: 107 us
  Pallas kernels  107 us (100%)
    pallas_call x1, Pallas kernels, per_device(): pl.pallas_call(kernel, out_shape=(pltpu.VMEM((8, 128), F32), pltpu.VMEM((...  105 us

profile of v3, /device:TPU:1, one launch (start us, length us, event | category | flops | bytes accessed | tf_op | source)
XLA Modules:
  0.0 107.2 jit_solution(5337538253515385436)
XLA Ops:
  0.6 105.2 %shard_map.76 = (f32[8,128]{1,0:T(8,128)S(1)}, bf16[256,2048]{1,0:T(8,128)(2,1)S(1)}, f32[256,1024]{1,0:T(8,128)S(1)}) custom-call(s32[8,128]{1,0:T(8,128)} %bitcast.9, bf16[8,128]{1,0:T(8,128)(2,1)} %bitcast.10, bf16[128,4096]{1,0:T(8,128)(2,1)} %og_hbm.1, bf16[256,2048]{1,0:T(8,128)(2,1)} %bitcast.7, bf16[256,1024]{1,0:T(8,128)(2,1)} %bitcast.8), custom_call_target="tpu_custom_call" | custom-call | tf_op jit(solution)/shard_map/pallas_call | solution.py:470
  105.9 1.3 %shard_map.77 = (f32[8,128]{1,0:T(8,128)}, bf16[256,2048]{1,0:T(8,128)(2,1)}, f32[256,1024]{1,0:T(8,128)}) custom-call(f32[8,128]{1,0:T(8,128)S(1)} %get-tuple-element.9.dp, bf16[256,2048]{1,0:T(8,128)(2,1)S(1)} %get-tuple-element.10.gp, f32[256,1024]{1,0:T(8,128)S(1)} %get-tuple-element.11.gd), custom_call_target="tpu_custom_call" | custom-call | tf_op jit(solution)/shard_map/pallas_call | solution.py:533

commit v4 on v3

--- a/solution.py
+++ b/solution.py
@@ -172,6 +172,16 @@
         gbuf[d] = pick.reshape(ne * CAP, 128).astype(BF16)
     wsend[...] = wacc.astype(BF16)
 
+    for_away(lambda to: drain(wrows(act, to), as_r.at[to]))
+    for d in (2, 1, 3):
+        remote(
+            act.at[pl.ds(0, 256)],
+            act.at[pl.ds((4 - d) * 256, 256)],
+            act_s.at[d],
+            act_r.at[4 - d],
+            at_x(d),
+        ).start()
+
     def expand(h):
         for d in (0, 1, 3, 2):
             drain(ogb.at[d, h], og_r.at[h, d])
@@ -222,16 +232,6 @@
     expand(1)
     exchange(0, 1)
     exchange(*ISSUE[0])
-
-    for_away(lambda to: drain(wrows(act, to), as_r.at[to]))
-    for d in (2, 1, 3):
-        remote(
-            act.at[pl.ds(0, 256)],
-            act.at[pl.ds((4 - d) * 256, 256)],
-            act_s.at[d],
-            act_r.at[4 - d],
-            at_x(d),
-        ).start()
 
     drain(wq.at[0, pl.ds(0, 256), :], w_r.at[1])
     remote(
@@ -344,60 +344,66 @@
     for d in range(3):
         drain(brecv.at[d], b_r.at[d])
 
-    def sum_x(i, carry):
-        rows = pl.ds(pl.multiple_of(i * CAP, CAP), CAP)
+    def sum_rows(to):
+        rows = pl.ds(pl.multiple_of(to * CAP, CAP), CAP)
         back = bp[0, rows, :] + brecv[0, rows, :].astype(F32)
-        back = back + brecv[1, rows, :].astype(F32) + brecv[2, rows, :].astype(F32)
-        bp[0, rows, :] = back
-
-        @pl.when(away(i) == 1)
-        def _():
-            bgive[rows, :] = back.astype(BF16)
-            remote(
-                wrows(bgive, i), wrows(btake, i), bs_s.at[i], bs_r.at[i], z_peer
-            ).start()
-
-        return carry
-
-    lax.fori_loop(0, ne, sum_x, 0)
+        return rows, back + brecv[1, rows, :].astype(F32) + brecv[2, rows, :].astype(F32)
+
+    def give(to):
+        rows, back = sum_rows(to)
+        bgive[rows, :] = back.astype(BF16)
+        remote(wrows(bgive, to), wrows(btake, to), bs_s.at[to], bs_r.at[to], z_peer).start()
+
+    for_away(give)
     for p in range(ZFIRST, ZPARTS):
         start_z(p)
 
-    def take(to):
+    def finish(to, rows, back, weight):
+        slot_grad = jnp.sum(acth[rows, :].astype(F32) * back, axis=1, keepdims=True)
+        sgb[rows, :] = jnp.broadcast_to(slot_grad, (CAP, 128))
+        bp[0, rows, :] = weight.astype(F32) * back
+
+    def send_back(to):
+        remote(wrows(sgb, to), wrows(ret, e), ret_s, ret_r, (f, to)).start()
+
+    def finish_home(to, carry):
+        @pl.when(away(to) == 0)
+        def _():
+            rows, back = sum_rows(to)
+            finish(to, rows, back, wbuf[rows, 0:1])
+
+            @pl.when(to != e)
+            def _():
+                send_back(to)
+
+        return carry
+
+    lax.fori_loop(0, ne, finish_home, 0)
+    pltpu.make_async_copy(wrows(sgb, e), wrows(ret, e), ret_r).start()
+
+    def grad_pre(rows):
+        hidden = bp[0, rows, :]
+        gp_out[rows, 0:1024] = (hidden * bvec[rows, 0:1024]).astype(BF16)
+        gp_out[rows, 1024:2048] = (hidden * bvec[rows, 1024:2048]).astype(BF16)
+
+    def grad_pre_home(to, carry):
+        @pl.when(away(to) == 0)
+        def _():
+            grad_pre(pl.ds(pl.multiple_of(to * CAP, CAP), CAP))
+
+        return carry
+
+    lax.fori_loop(0, ne, grad_pre_home, 0)
+
+    def finish_away(to):
         rows = pl.ds(pl.multiple_of(to * CAP, CAP), CAP)
         drain(wrows(btake, to), bs_r.at[to])
         drain(wrows(wswap, to), ws_r.at[to])
-        bp[0, rows, :] = btake[rows, :].astype(F32)
-
-    def finish(i, carry):
-        rows = pl.ds(pl.multiple_of(i * CAP, CAP), CAP)
-        back = bp[0, rows, :]
-        slot_grad = jnp.sum(acth[rows, :].astype(F32) * back, axis=1, keepdims=True)
-        sgb[rows, :] = jnp.broadcast_to(slot_grad, (16, 128))
-        weight = jnp.where(away(i) == 1, wswap[rows, 0:1].astype(F32), wbuf[rows, 0:1].astype(F32))
-        bp[0, rows, :] = weight * back
-        return carry
-
-    for_away(take)
-    lax.fori_loop(0, ne, finish, 0)
-
-    pltpu.make_async_copy(wrows(sgb, e), wrows(ret, e), ret_r).start()
-
-    def send_back(k, carry):
-        to = (e + k) % ne
-        remote(wrows(sgb, to), wrows(ret, e), ret_s, ret_r, (f, to)).start()
-        return carry
-
-    lax.fori_loop(1, ne, send_back, 0)
-
-    def grad_pre(i, carry):
-        rows = pl.ds(pl.multiple_of(i * 16, 16), 16)
-        hidden = bp[0, rows, :]
-        gp_out[rows, 0:1024] = (hidden * bvec[rows, 0:1024]).astype(BF16)
-        gp_out[rows, 1024:2048] = (hidden * bvec[rows, 1024:2048]).astype(BF16)
-        return carry
-
-    lax.fori_loop(0, 16, grad_pre, 0)
+        finish(to, rows, btake[rows, :].astype(F32), wswap[rows, 0:1])
+        send_back(to)
+
+    for_away(finish_away)
+    for_away(lambda to: grad_pre(pl.ds(pl.multiple_of(to * CAP, CAP), CAP)))
 
     drain(crecv.at[1], c_r.at[1])
 

time: 107 us -> 105 us (0.981)
  Pallas kernels: 107 us -> 105 us
    pallas_call x1, Pallas kernels: 105 us -> 103 us  [per_device(): pl.pallas_call(kernel, out_shape=(pltpu.VMEM((8, 128), F32), pltpu.VMEM((...]
where the time goes in v4:
time: 105 us
  Pallas kernels  105 us (100%)
    pallas_call x1, Pallas kernels, per_device(): pl.pallas_call(kernel, out_shape=(pltpu.VMEM((8, 128), F32), pltpu.VMEM((...  103 us

profile of v4, /device:TPU:1, one launch (start us, length us, event | category | flops | bytes accessed | tf_op | source)
XLA Modules:
  0.0 105.2 jit_solution(3861968879065639459)
XLA Ops:
  0.6 103.2 %shard_map.76 = (f32[8,128]{1,0:T(8,128)S(1)}, bf16[256,2048]{1,0:T(8,128)(2,1)S(1)}, f32[256,1024]{1,0:T(8,128)S(1)}) custom-call(s32[8,128]{1,0:T(8,128)} %bitcast.9, bf16[8,128]{1,0:T(8,128)(2,1)} %bitcast.10, bf16[128,4096]{1,0:T(8,128)(2,1)} %og_hbm.1, bf16[256,2048]{1,0:T(8,128)(2,1)} %bitcast.7, bf16[256,1024]{1,0:T(8,128)(2,1)} %bitcast.8), custom_call_target="tpu_custom_call" | custom-call | tf_op jit(solution)/shard_map/pallas_call | solution.py:476
  103.9 1.3 %shard_map.77 = (f32[8,128]{1,0:T(8,128)}, bf16[256,2048]{1,0:T(8,128)(2,1)}, f32[256,1024]{1,0:T(8,128)}) custom-call(f32[8,128]{1,0:T(8,128)S(1)} %get-tuple-element.9.dp, bf16[256,2048]{1,0:T(8,128)(2,1)S(1)} %get-tuple-element.10.gp, f32[256,1024]{1,0:T(8,128)S(1)} %get-tuple-element.11.gd), custom_call_target="tpu_custom_call" | custom-call | tf_op jit(solution)/shard_map/pallas_call | solution.py:539

commit v5 on v4

--- a/solution.py
+++ b/solution.py
@@ -13,9 +13,9 @@
 STAGES = ((0, 1, 3), (1, 2, 1), (1, 1, 1), (1, 3, 1), (0, 0, 1), (1, 0, 1))
 WSTAGE = len(STAGES)
 ISSUE = ((1, 5), (6, 0), (6, 0))
-ZPARTS = 8
-ZFIRST = 5
-ZROWS = 256 // ZPARTS
+ZROWS = ((0, 160), (160, 96))
+ZPARTS = 2
+ZFIRST = 1
 
 
 def kernel(
@@ -309,7 +309,7 @@
             ).start()
 
     def start_z(p):
-        part = pl.ds(p * ZROWS, ZROWS)
+        part = pl.ds(*ZROWS[p])
         remote(zsend.at[part], zrecv.at[part], z_s.at[p], z_r.at[p], z_peer).start()
 
     arrived(0)
@@ -430,8 +430,8 @@
     dp_out[...] = dp
 
     for p in range(ZPARTS):
-        drain(zrecv.at[pl.ds(p * ZROWS, ZROWS)], z_r.at[p])
-        lax.fori_loop(p * ZROWS // 16, (p + 1) * ZROWS // 16, total, 0)
+        drain(zrecv.at[pl.ds(*ZROWS[p])], z_r.at[p])
+        lax.fori_loop(ZROWS[p][0] // 16, sum(ZROWS[p]) // 16, total, 0)
 
     def left(to):
         drain(wrows(acth, to), as_s.at[to])
@@ -450,7 +450,7 @@
     for h in range(2):
         drain(csend.at[h], c_s.at[h])
     for p in range(ZPARTS):
-        drain(zsend.at[pl.ds(p * ZROWS, ZROWS)], z_s.at[p])
+        drain(zsend.at[pl.ds(*ZROWS[p])], z_s.at[p])
     for i, (h, d0, dn) in enumerate(STAGES):
         drain(sendbuf.at[h, pl.ds(d0, dn), pl.ds(0, (ne - 1) * CAP), :], a_s.at[i])
     drain(wsend.at[pl.ds(0, (ne - 1) * CAP)], a_s.at[WSTAGE])

time: 105 us -> 105 us (level)
  no operation moved by 1% of the time
where the time goes in v5:
time: 105 us
  Pallas kernels  104 us (99%)
    pallas_call x1, Pallas kernels, per_device(): pl.pallas_call(kernel, out_shape=(pltpu.VMEM((8, 128), F32), pltpu.VMEM((...  103 us

profile of v5, /device:TPU:1, one launch (start us, length us, event | category | flops | bytes accessed | tf_op | source)
XLA Modules:
  0.0 105.1 jit_solution(13676211131663910867)
XLA Ops:
  0.6 103.1 %shard_map.76 = (f32[8,128]{1,0:T(8,128)S(1)}, bf16[256,2048]{1,0:T(8,128)(2,1)S(1)}, f32[256,1024]{1,0:T(8,128)S(1)}) custom-call(s32[8,128]{1,0:T(8,128)} %bitcast.9, bf16[8,128]{1,0:T(8,128)(2,1)} %bitcast.10, bf16[128,4096]{1,0:T(8,128)(2,1)} %og_hbm.1, bf16[256,2048]{1,0:T(8,128)(2,1)} %bitcast.7, bf16[256,1024]{1,0:T(8,128)(2,1)} %bitcast.8), custom_call_target="tpu_custom_call" | custom-call | tf_op jit(solution)/shard_map/pallas_call | solution.py:476
  103.7 1.3 %shard_map.77 = (f32[8,128]{1,0:T(8,128)}, bf16[256,2048]{1,0:T(8,128)(2,1)}, f32[256,1024]{1,0:T(8,128)}) custom-call(f32[8,128]{1,0:T(8,128)S(1)} %get-tuple-element.9.dp, bf16[256,2048]{1,0:T(8,128)(2,1)S(1)} %get-tuple-element.10.gp, f32[256,1024]{1,0:T(8,128)S(1)} %get-tuple-element.11.gd), custom_call_target="tpu_custom_call" | custom-call | tf_op jit(solution)/shard_map/pallas_call | solution.py:539
